TPU v7x, 32 devices: a whole 2x2x4 slice. The times are simulated.
32 devices in a mesh: dp: 4 (over y, x), seq: 8 (over z, core).
Axes of the slice: x: 2, y: 2, z: 4, core: 2. Of those that a mesh axis runs over, the one named last changes fastest.
Arguments:
- hidden: bfloat16 [8, 1536, 3072], P('dp', 'seq'), may hold values from -6 to 6
- cotangent: bfloat16 [8, 1536, 1536], P('dp', 'seq'), may hold values from -6 to 6
- lengths: int32 [8], P('dp'), may hold values from 192 to 1536, as said below
- kernel: float32 [1536, 31], replicated, may hold values from -1 to 1
- conv_gain: float32 [1536], replicated, may hold values from 0.1 to 1.9
- w_out: bfloat16 [1536, 1536], replicated, may hold values from -0.15625 to 0.15625
Outputs:
- grad_hidden: bfloat16 [8, 1536, 3072], P('dp', 'seq')
- grad_w_out: float32 [1536, 1536], P(('dp', 'seq'))
- grad_kernel: float32 [1536, 31], P(('dp', 'seq'))
- grad_conv_gain: float32 [1536], P(('dp', 'seq'))
Inputs may be any that keep to these rules, and one draw needn't show every extreme that they name: `lengths`: the first utterance of every group of 2 on one index of dp fills all 1536 frames.
All inputs are finite; a program needn't handle non-finite values.
Results may differ from a plain program's by a relative error of at most 0.0055.
Values may be sent and summed in bfloat16 or wider, within the bound.
A program may use at most 128 MiB of HBM per device.

v0:
```python
import math

import jax
import jax.numpy as jnp
from jax import lax
from jax.sharding import PartitionSpec as P

EPSILON = 1e-05


def extended(cells, sides, width):
    for axis, dim in sides:
        count = lax.axis_size(axis)
        ends = count - 1
        head = lax.slice_in_dim(cells, 0, width, axis=dim)
        tail = lax.slice_in_dim(cells, cells.shape[dim] - width, cells.shape[dim], axis=dim)
        cells = jnp.concatenate(
            [
                lax.ppermute(tail, axis, [(i, (i + 1) % count) for i in range(ends)]),
                cells,
                lax.ppermute(head, axis, [((i + 1) % count, i) for i in range(ends)]),
            ],
            axis=dim,
        )
    return cells


def normalize(values):
    centered = values - jnp.mean(values, axis=-1, keepdims=True)
    inverse = lax.rsqrt(jnp.mean(centered * centered, axis=-1, keepdims=True) + EPSILON)
    return (centered * inverse, inverse)


def norm_backward(grad_hat, normed, inverse):
    return inverse * (
        grad_hat
        - jnp.mean(grad_hat, axis=-1, keepdims=True)
        - normed * jnp.mean(grad_hat * normed, axis=-1, keepdims=True)
    )


def inner_rows(left_side, right_side):
    return lax.dot_general(
        left_side, right_side, (((0,), (0,)), ((), ())), preferred_element_type=jnp.float32
    )


def outer_cols(left_side, right_side):
    return lax.dot_general(
        left_side, right_side, (((1,), (1,)), ((), ())), preferred_element_type=jnp.float32
    )


def depthwise(padded, kernel, length):
    result = padded[:, 0:length] * kernel[:, 0]
    for offset in range(1, kernel.shape[1]):
        result = result + padded[:, offset : offset + length] * kernel[:, offset]
    return result


def transposed(grad_padded, kernel, length):
    last_tap = kernel.shape[1] - 1
    result = grad_padded[:, last_tap : last_tap + length] * kernel[:, 0]
    for offset in range(1, kernel.shape[1]):
        result = (
            result
            + grad_padded[:, last_tap - offset : last_tap - offset + length] * kernel[:, offset]
        )
    return result


def kernel_terms(grad_float, padded, length, kernel_taps):
    return jnp.stack(
        [
            jnp.sum(grad_float * padded[:, offset : offset + length], axis=(0, 1))
            for offset in range(kernel_taps)
        ],
        axis=1,
    )


def local(hidden, cotangent, lengths, kernel, conv_gain, w_out):
    groups, frames, double_width = hidden.shape
    model_width = double_width // 2
    kernel_taps = kernel.shape[1]
    half_width = kernel_taps // 2
    seq_count = lax.axis_size("seq")
    row_total = groups * frames
    positions = lax.axis_index("seq") * frames + jnp.arange(frames, dtype=jnp.int32)
    valid_frames = (positions[None, :] < lengths[:, None]).astype(jnp.float32)
    valid_rows = valid_frames.reshape(row_total, 1)
    hidden_rows = hidden.reshape(row_total, double_width).astype(jnp.float32)
    linear = hidden_rows[:, :model_width]
    gate_open = jax.nn.sigmoid(hidden_rows[:, model_width:])
    glu_out = (linear * gate_open * valid_rows).astype(jnp.bfloat16)
    glu_block = glu_out.reshape(groups, frames, model_width)
    padded = extended(glu_block, (("seq", 1),), half_width).astype(jnp.float32)
    conv_out = depthwise(padded, kernel, frames)
    conv_hat, conv_inverse = normalize(conv_out.reshape(row_total, model_width))
    pre_act = conv_hat * conv_gain
    act_gate = jax.nn.sigmoid(pre_act)
    swished = (pre_act * act_gate).astype(jnp.bfloat16)
    grad_out = (cotangent * valid_frames.astype(jnp.bfloat16)[:, :, None]).reshape(
        row_total, model_width
    )
    grad_swish = outer_cols(grad_out, w_out)
    grad_pre = grad_swish * act_gate * (1.0 + pre_act * (1.0 - act_gate))
    term_conv = jnp.sum(grad_pre * conv_hat, axis=0)
    grad_conv = norm_backward(grad_pre * conv_gain, conv_hat, conv_inverse).astype(jnp.bfloat16)
    grad_block = grad_conv.reshape(groups, frames, model_width)
    grad_padded = extended(grad_block, (("seq", 1),), half_width).astype(jnp.float32)
    grad_glu = transposed(grad_padded, kernel, frames)
    term_kernel = kernel_terms(grad_block.astype(jnp.float32), padded, frames, kernel_taps)
    grad_glu = grad_glu.reshape(row_total, model_width) * valid_rows
    grad_local = jnp.concatenate(
        [grad_glu * gate_open, grad_glu * linear * gate_open * (1.0 - gate_open)], axis=1
    ).astype(jnp.bfloat16)
    count_all = groups * lax.axis_size("dp") * frames * seq_count
    factor = 1.0 / math.sqrt(count_all)
    term_out = inner_rows(swished, grad_out)
    sum_out, sum_kernel, sum_conv = (
        lax.psum_scatter(term_out, ("dp", "seq"), scatter_dimension=0, tiled=True),
        lax.psum_scatter(term_kernel, ("dp", "seq"), scatter_dimension=0, tiled=True),
        lax.psum_scatter(term_conv, ("dp", "seq"), scatter_dimension=0, tiled=True),
    )
    grad_hidden = grad_local.reshape(groups, frames, double_width)
    return (grad_hidden, sum_out * factor, sum_kernel * factor, sum_conv * factor)


def solution(mesh):
    in_specs = (P("dp", "seq", None), P("dp", "seq", None), P("dp"), P(), P(), P())
    out_specs = (
        P("dp", "seq", None),
        P(("dp", "seq"), None),
        P(("dp", "seq"), None),
        P(("dp", "seq")),
    )
    return jax.shard_map(local, mesh=mesh, in_specs=in_specs, out_specs=out_specs, check_vma=False)
```

profile of v0, /device:TPU:0, one launch (start us, length us, event | category | flops | bytes accessed | tf_op | source)
XLA Modules:
  0.0 302.1 jit_solution(7304403424927797502)
XLA Ops:
  8.0 2.2 bitcast_convert_fusion
  10.9 1.6 copy-done
  12.5 2.4 collective-permute-start
  14.9 1.3 collective-permute-start.1
  16.5 1.2 broadcast_multiply_fusion
  17.9 2.3 collective-permute-done.1
  20.7 11.5 %fusion.72 = (f32[2,192]{1,0:T(2,128)S(1)}, f32[2,192,1536]{2,1,0:T(8,128)}) fusion(f32[1536]{0:T(1024)S(1)} %get-tuple-element.67, f32[2,222,1536]{2,1,0:T(8,128)S(1)} %maximum_convert_fusion, f32[1536]{0:T(1024)S(1)} %get-tuple-element.68, f32[1536]{0:T(1024)S(1)} %get-tuple-element.39, f32[1536]{0:T(1024)S(1)} %get-tuple-element.40, ...), kind=kLoop, calls=%fused_computation.194 | loop fusion | flops 36568704 | bytes 75689472 | tf_op jit(solution)/shard_map/reduce_sum | solution.py:29
  32.3 2.0 multiply_reduce_fusion.2
  34.5 2.1 fusion.65
  37.2 4.8 %multiply_reduce_fusion = (f32[1536]{0:T(1024)S(1)}, f32[384]{0:T(512)S(1)}, f32[384]{0:T(512)S(1)}, f32[384,1536]{1,0:T(8,128)S(1)}) fusion(f32[2,192,1536]{2,1,0:T(8,128)S(1)} %copy-done.1, f32[384]{0:T(512)S(1)} %div.26, f32[384]{0:T(512)S(1)} %rsqrt.13, f32[1536]{0:T(1024)S(1)} %copy-done.8, f32[384,1536]{1,0:T(8,128)S(1)} %fusion.65, ...), kind=kOutput, calls=%fused_computation.135 | convolution fusion | flops 1821964032 | bytes 12994560 | tf_op jit(solution)/shard_map/dot_general | solution.py:49
  42.7 4.0 %fusion.30 = (f32[1536]{0:T(1024)S(1)}, f32[1536]{0:T(1024)S(1)}, f32[1536]{0:T(1024)S(1)}, f32[1536]{0:T(1024)S(1)}, f32[1536]{0:T(1024)S(1)}, /*index=5*/f32[1...) fusion(bf16[2,192,1536]{2,1,0:T(8,128)(2,1)S(1)} %bitcast.32, ...), kind=kLoop, calls=%fused_computation.63 | loop fusion | flops 15905280 | bytes 31930368 | tf_op jit(solution)/shard_map/reduce_sum | solution.py:75
  46.7 5.6 %fusion.31 = (f32[1536]{0:T(1024)S(1)}, f32[1536]{0:T(1024)S(1)}, f32[1536]{0:T(1024)S(1)}, f32[1536]{0:T(1024)S(1)}, f32[1536]{0:T(1024)S(1)}, /*index=5*/f32[1...) fusion(bf16[2,192,1536]{2,1,0:T(8,128)(2,1)S(1)} %bitcast.33, ...), kind=kLoop, calls=%fused_computation.64 | loop fusion | flops 21795840 | bytes 43757568 | tf_op jit(solution)/shard_map/reduce_sum | solution.py:75
  53.0 1.2 copy.10
  54.5 6.6 %convolution_bitcast_fusion = f32[1536,1536]{1,0:T(8,128)} fusion(bf16[2,192,1536]{2,1,0:T(8,128)(2,1)} %broadcast_multiply_fusion, f32[2,192,1536]{2,1,0:T(8,128)S(1)} %copy-done.2, f32[1536]{0:T(1024)S(1)} %copy-done.8, f32[2,192]{1,0:T(2,128)S(1)} %add_rsqrt_fusion, f32[2,192]{1,0:T(2,128)S(1)} %broadcast_multiply_fusion.5), kind=kOutput, calls=%fused_computation.31 | convolution fusion | flops 1816657920 | bytes 12985344 | tf_op jit(solution)/shard_map/dot_general | solution.py:43
  61.2 1.2 copy-done.4
  62.5 5.2 %collective-permute-start.2 = (bf16[2,15,1536]{2,1,0:T(8,128)(2,1)S(1)}, bf16[2,15,1536]{2,1,0:T(8,128)(2,1)S(1)}, u32[]{:S(2)}, u32[]{:S(2)}) collective-permute-start(bf16[2,15,1536]{2,1,0:T(8,128)(2,1)S(1)} %get-tuple-element.73), channel_id=1, source_target_pairs={{0,1},{1,2},{2,3},{3,4},{4,5},{5,6},{6,7},{8,9},{9,10},{10,11},{11... | collective-permute-start | bytes 276488 | tf_op jit(solution)/shard_map/ppermute | solution.py:19
  67.6 1.3 collective-permute-start.3
  68.9 41.3 %all-reduce = f32[1536]{0:T(1024)S(1)} all-reduce(f32[1536]{0:T(1024)S(1)} %get-tuple-element.4), channel_id=4, replica_groups=mesh['dp'=4,'seq'=8] {'dp','seq'}, use_global_device_ids=true, to_apply=%region_38.0.clone | all-reduce | flops 1536 | bytes 12288
  111.3 9.0 %fusion.32 = f32[2,192,1536]{2,1,0:T(8,128)S(1)} fusion(f32[2,222,1536]{2,1,0:T(8,128)S(1)} %maximum_convert_fusion.1, f32[1536]{0:T(1024)S(1)} %get-tuple-element.67, f32[1536]{0:T(1024)S(1)} %get-tuple-element.68, f32[1536]{0:T(1024)S(1)} %get-tuple-element.39, f32[1536]{0:T(1024)S(1)} %get-tuple-element.40, f32[1536]{0:T(1024)S(1)} %get-tuple-element.41, ...), kind=kLoop, calls=%fused_computation.66 | loop fusion | flops 35979264 | bytes 75687936 | tf_op jit(solution)/shard_map/add | solution.py:66
  120.3 1.4 multiply_convert_fusion.2
  121.7 1.7 pad_maximum_fusion
  123.4 29.6 %reduce-scatter.7.cloned.1.call-done = f32[48,31]{1,0:T(8,128)} async-done(((f32[1536,31]{1,0:T(8,128)}), f32[48,31]{1,0:T(8,128)}) %reduce-scatter.7.cloned.1.call-update) | async-done | bytes 5968
  154.4 139.2 %reduce-scatter.5.cloned.1.call-done = f32[48,1536]{1,0:T(8,128)} async-done(((f32[1536,1536]{1,0:T(8,128)}), f32[48,1536]{1,0:T(8,128)}) %reduce-scatter.5.cloned.1.call-update) | async-done | bytes 294928 | tf_op jit(solution)/shard_map/reduce_scatter | solution.py:122
  293.6 1.7 broadcast_multiply_fusion.1
  (79 shorter events, 7.2 us)
Async XLA Ops:
  7.2 145.8 %reduce-scatter.7.cloned.1.call-start = ((), (), s32[]{:S(2)}) async-start(), calls=%async_computation.3 | async-start | bytes 811008
  10.3 2.2 copy-start
  10.3 5.9 %copy-start.7 = (f32[1536,31]{0,1:T(8,128)S(1)}, f32[1536,31]{0,1:T(8,128)}, u32[]{:S(2)}) copy-start(f32[1536,31]{0,1:T(8,128)} %param.9) | copy-start | bytes 571396
  10.3 6.2 %copy-start.5 = (bf16[2,192,1536]{2,1,0:T(8,128)(2,1)S(1)}, bf16[2,192,1536]{2,1,0:T(8,128)(2,1)}, u32[]{:S(2)}) copy-start(bf16[2,192,1536]{2,1,0:T(8,128)(2,1)} %param.7) | copy-start | bytes 3538948
  12.5 5.4 %collective-permute-start = (bf16[2,15,1536]{2,1,0:T(8,128)(2,1)S(1)}, bf16[2,15,1536]{2,1,0:T(8,128)(2,1)S(1)}, u32[]{:S(2)}, u32[]{:S(2)}) collective-permute-start(bf16[2,15,1536]{2,1,0:T(8,128)(2,1)S(1)} %get-tuple-element.75), channel_id=1, source_target_pairs={{0,1},{1,2},{2,3},{3,4},{4,5},{5,6},{6,7},{8,9},{9,10},{10,11},{11... | collective-permute-start | bytes 276488 | tf_op jit(solution)/shard_map/ppermute | solution.py:19
  14.9 5.4 %collective-permute-start.1 = (bf16[2,15,1536]{2,1,0:T(8,128)(2,1)S(1)}, bf16[2,15,1536]{2,1,0:T(8,128)(2,1)S(1)}, u32[]{:S(2)}, u32[]{:S(2)}) collective-permute-start(bf16[2,15,1536]{2,1,0:T(8,128)(2,1)S(1)} %get-tuple-element.76), channel_id=1, source_target_pairs={{1,0},{2,1},{3,2},{4,3},{5,4},{6,5},{7,6},{9,8},{10,9},{11,10},{12... | collective-permute-start | bytes 276488 | tf_op jit(solution)/shard_map/ppermute | solution.py:21
  34.4 2.4 copy-start.1
  34.4 2.7 copy-start.6
  34.5 2.7 copy-start.8
  42.7 4.0 %copy-start.3 = (bf16[384,1536]{1,0:T(8,128)(2,1)}, bf16[384,1536]{1,0:T(8,128)(2,1)S(1)}, u32[]{:S(2)}) copy-start(bf16[384,1536]{1,0:T(8,128)(2,1)S(1)} %multiply_convert_fusion.3) | copy-start | bytes 3538948
  52.3 2.2 copy-start.2
  54.3 239.3 %reduce-scatter.5.cloned.1.call-start = ((), (), s32[]{:S(2)}) async-start(), calls=%async_computation.2 | async-start | bytes 9732096 | tf_op jit(solution)/shard_map/reduce_scatter | solution.py:122
  61.2 1.3 copy-start.4
  62.5 48.4 %collective-permute-start.2 = (bf16[2,15,1536]{2,1,0:T(8,128)(2,1)S(1)}, bf16[2,15,1536]{2,1,0:T(8,128)(2,1)S(1)}, u32[]{:S(2)}, u32[]{:S(2)}) collective-permute-start(bf16[2,15,1536]{2,1,0:T(8,128)(2,1)S(1)} %get-tuple-element.73), channel_id=1, source_target_pairs={{0,1},{1,2},{2,3},{3,4},{4,5},{5,6},{6,7},{8,9},{9,10},{10,11},{11... | collective-permute-start | bytes 276488 | tf_op jit(solution)/shard_map/ppermute | solution.py:19
  67.6 43.2 %collective-permute-start.3 = (bf16[2,15,1536]{2,1,0:T(8,128)(2,1)S(1)}, bf16[2,15,1536]{2,1,0:T(8,128)(2,1)S(1)}, u32[]{:S(2)}, u32[]{:S(2)}) collective-permute-start(bf16[2,15,1536]{2,1,0:T(8,128)(2,1)S(1)} %get-tuple-element.74), channel_id=1, source_target_pairs={{1,0},{2,1},{3,2},{4,3},{5,4},{6,5},{7,6},{9,8},{10,9},{11,10},{12... | collective-permute-start | bytes 276488 | tf_op jit(solution)/shard_map/ppermute | solution.py:21
  110.8 9.4 %slice-start = ((s8[4718592]{0:T(1024)(128)(4,1)}), s8[4194304]{0:T(1024)(128)(4,1)S(1)}, s32[]{:S(2)}) async-start(s8[4718592]{0:T(1024)(128)(4,1)} %bitcast.30), calls=%async_computation.4 | async-start | bytes 8388608
  111.2 9.0 %slice-start.1 = ((s8[4718592]{0:T(1024)(128)(4,1)}), s8[524288]{0:T(1024)(128)(4,1)S(1)}, s32[]{:S(2)}) async-start(s8[4718592]{0:T(1024)(128)(4,1)} %bitcast.30), calls=%async_computation.5 | async-start | bytes 1048576
Sparse Core Ops, SparseCore 0:
  54.4 98.5 reduce-scatter.6
  158.9 134.6 reduce-scatter.4
where the time goes:
time: 303 us; the launch traced here: 302 us
  waiting for transfers between devices  171 us (56%)
  other arithmetic  46.5 us (15%)
  blocking collectives  41.3 us (14%)
  between operations  14.6 us (5%)
  matrix products  11.5 us (4%)
  starting transfers between devices  10.4 us (3%)
  local copies, waits for them, and re-layouts  6.78 us (2%)
    reduce_scatter x1, waiting for transfers between devices, local(): lax.psum_scatter(term_out, ('dp', 'seq'), scatter_dimension=0, tiled=True)  139 us
    unnamed x1, blocking collectives  41.3 us
    unnamed x3, waiting for transfers between devices  29.6 us
    reduce_sum x1, other arithmetic, normalize(): centered = values - jnp.mean(values, axis=-1, keepdims=True)  11.5 us
    reduce_sum x2, other arithmetic, kernel_terms(): jnp.sum(grad_float * padded[:, offset:offset + length], axis=(0, 1))  9.52 us
    add x1, other arithmetic, transposed(): result + grad_padded[:, last_tap - offset:last_tap - offset + length] * k...  9.01 us
    ppermute x2, starting transfers between devices, extended(): lax.ppermute(tail, axis, [(i, (i + 1) % count) for i in range(ends)])  7.52 us
    dot_general x1, matrix products, inner_rows(): lax.dot_general(left_side, right_side, (((0,), (0,)), ((), ())), preferre...  6.64 us
  transfers between devices with their start and end apart: 6, of which 3 were waited for; matrix products, arithmetic and copies ran while one was open for 8% of the time, Pallas kernels for 0%

commit v1 on v0

v1 whole, which is shorter than its diff:
```python
import functools
import math

import jax
import jax.numpy as jnp
from jax import lax
from jax.experimental import pallas as pl
from jax.experimental.pallas import tpu as pltpu
from jax.sharding import PartitionSpec as P

EPSILON = 1e-05
LANES = 128
EDGE = 16
MESH = pl.DeviceIdType.MESH
VMEM_LIMIT = 56 * 2**20


def sigmoid(x):
    return jax.nn.sigmoid(x)


def chunk_of(frames):
    return 64 if frames % 64 == 0 else 32 if frames % 32 == 0 else 16


def forward_kernel(taps, lin_ref, gate_ref, left_ref, right_ref, valid_ref, taps_ref, gain_ref,
                   up_ref, swished_ref, grad_ref, term_ref, ext, conv):
    groups, frames, _ = lin_ref.shape
    blocks = conv.shape[0]
    width = blocks * LANES
    half = taps // 2
    block = pl.program_id(0)
    chunk = chunk_of(frames)
    for u in range(groups):
        gated = (
            lin_ref[u].astype(jnp.float32) * sigmoid(gate_ref[u].astype(jnp.float32)) * valid_ref[u]
        ).astype(jnp.bfloat16)
        ext[u, pl.ds(0, EDGE), :] = left_ref[u].astype(jnp.float32)
        ext[u, pl.ds(EDGE, frames), :] = gated.astype(jnp.float32)
        ext[u, pl.ds(EDGE + frames, EDGE), :] = right_ref[u].astype(jnp.float32)
        for start in range(0, frames, chunk):
            total = jnp.zeros((chunk, LANES), jnp.float32)
            for tap in range(taps):
                total = total + ext[u, pl.ds(start + tap + EDGE - half, chunk), :] * taps_ref[
                    pl.ds(tap, 1), :
                ]
            conv[block, pl.ds(u * frames + start, chunk), :] = total

    @pl.when(block == blocks - 1)
    def _():
        rows = EDGE
        term_ref[...] = jnp.zeros_like(term_ref)
        inverse_width = 1.0 / width

        def part(index, _):
            span = pl.ds(pl.multiple_of(index * rows, rows), rows)
            values = [conv[b, span, :] for b in range(blocks)]
            mean = jnp.sum(sum(values), axis=-1, keepdims=True) * inverse_width
            values = [v - mean for v in values]
            square = jnp.sum(sum(v * v for v in values), axis=-1, keepdims=True) * inverse_width
            inverse = lax.rsqrt(square + EPSILON)
            first = jnp.zeros((rows, LANES), jnp.float32)
            second = jnp.zeros((rows, LANES), jnp.float32)
            for b in range(blocks):
                lanes = pl.ds(b * LANES, LANES)
                gain = gain_ref[:, lanes]
                hat = values[b] * inverse
                pre = hat * gain
                gate = sigmoid(pre)
                swished_ref[span, lanes] = (pre * gate).astype(jnp.bfloat16)
                grad_pre = up_ref[span, lanes] * gate * (1.0 + pre * (1.0 - gate))
                product = grad_pre * hat
                term_ref[:, lanes] += product[:8] + product[8:]
                grad = grad_pre * gain
                first = first + grad
                second = second + grad * hat
                conv[b, span, :] = grad
                values[b] = hat
            mean_first = jnp.sum(first, axis=-1, keepdims=True) * inverse_width
            mean_second = jnp.sum(second, axis=-1, keepdims=True) * inverse_width
            for b in range(blocks):
                lanes = pl.ds(b * LANES, LANES)
                result = inverse * (conv[b, span, :] - mean_first - values[b] * mean_second)
                grad_ref[span, lanes] = result.astype(jnp.bfloat16)
            return 0

        lax.fori_loop(0, groups * frames // rows, part, 0)


def forward(hidden, left, right, valid, taps_rows, gain, upstream, taps):
    groups, frames, double = hidden.shape
    width = double // 2
    blocks = width // LANES
    rows = groups * frames
    whole = lambda shape: pl.BlockSpec(shape, lambda b: (0,) * len(shape))
    return pl.pallas_call(
        functools.partial(forward_kernel, taps),
        grid=(blocks,),
        in_specs=[
            pl.BlockSpec((groups, frames, LANES), lambda b: (0, 0, b)),
            pl.BlockSpec((groups, frames, LANES), lambda b: (0, 0, b + blocks)),
            pl.BlockSpec((groups, EDGE, LANES), lambda b: (0, 0, b)),
            pl.BlockSpec((groups, EDGE, LANES), lambda b: (0, 0, b)),
            whole((groups, frames, LANES)),
            pl.BlockSpec((taps_rows.shape[0], LANES), lambda b: (0, b)),
            whole((1, width)),
            whole((rows, width)),
        ],
        out_specs=[whole((rows, width)), whole((rows, width)), whole((8, width))],
        out_shape=[
            jax.ShapeDtypeStruct((rows, width), jnp.bfloat16),
            jax.ShapeDtypeStruct((rows, width), jnp.bfloat16),
            jax.ShapeDtypeStruct((8, width), jnp.float32),
        ],
        scratch_shapes=[
            pltpu.VMEM((groups, frames + 2 * EDGE, LANES), jnp.float32),
            pltpu.VMEM((blocks, rows, LANES), jnp.float32),
        ],
        compiler_params=pltpu.CompilerParams(vmem_limit_bytes=VMEM_LIMIT),
    )(hidden, hidden, left, right, valid, taps_rows, gain, upstream)


def orders_of(dp, seq):
    seq_bits, dp_bits = seq.bit_length() - 1, dp.bit_length() - 1
    others = list(range(seq_bits, seq_bits + dp_bits)) + list(range(1, seq_bits))
    turns = (0, 1, dp_bits)
    return [[0] + others[t:] + others[:t] for t in turns]


def place_of(index, order):
    place = 0
    for bit in order:
        place = place * 2 + (index >> bit) % 2
    return place


def backward_kernel(taps, dp, seq, reduce, factor, hidden_ref, grad_ref, swished_ref, out_ref, valid_ref,
                    taps_ref, hidden_grad_ref, sum_ref, term_ref, ext, gated, terms, halo, edge_send,
                    edge_recv, *scratch):
    groups, frames, double = hidden_ref.shape
    width = double // 2
    blocks = width // LANES
    half = taps // 2
    chunk = chunk_of(frames)
    my_dp, my_seq = lax.axis_index("dp"), lax.axis_index("seq")
    right = (my_dp, lax.rem(my_seq + 1, seq))
    left = (my_dp, lax.rem(my_seq + seq - 1, seq))
    seq_bits, dp_bits = seq.bit_length() - 1, dp.bit_length() - 1
    steps = seq_bits + dp_bits if reduce else 0

    def bit_of(bit):
        if bit < seq_bits:
            return lax.rem(my_seq // (1 << bit), 2)
        return lax.rem(my_dp // (1 << (bit - seq_bits)), 2)

    def partner_of(bit):
        turn = 1 - 2 * bit_of(bit)
        if bit < seq_bits:
            return (my_dp, my_seq + (1 << bit) * turn)
        return (my_dp + (1 << (bit - seq_bits)) * turn, my_seq)

    barrier = pltpu.get_barrier_semaphore()
    partners = [left, right] + [partner_of(b) for b in range(steps)]
    for device in partners:
        pl.semaphore_signal(barrier, inc=1, device_id=device, device_id_type=MESH)
    pl.semaphore_wait(barrier, len(partners))

    edges = []
    for u in range(groups):
        edges.append(pltpu.make_async_remote_copy(
            grad_ref.at[u, pl.ds(frames - EDGE, EDGE)], halo.at[0, u],
            edge_send.at[0, u], edge_recv.at[0, u], device_id=right, device_id_type=MESH))
        edges.append(pltpu.make_async_remote_copy(
            grad_ref.at[u, pl.ds(0, EDGE)], halo.at[1, u],
            edge_send.at[1, u], edge_recv.at[1, u], device_id=left, device_id_type=MESH))
    for copy in edges:
        copy.start()
    keep_left = jnp.where(my_seq == 0, 0.0, 1.0).astype(jnp.float32)
    keep_right = jnp.where(my_seq == seq - 1, 0.0, 1.0).astype(jnp.float32)

    def conv_block(block, _):
        lanes = pl.ds(pl.multiple_of(block * LANES, LANES), LANES)
        gate_lanes = pl.ds(pl.multiple_of(block * LANES + width, LANES), LANES)
        terms[...] = jnp.zeros_like(terms)

        def utterance(u, _):
            ext[pl.ds(0, EDGE), :] = halo[0, u, :, lanes].astype(jnp.float32) * keep_left
            ext[pl.ds(EDGE, frames), :] = grad_ref[u, :, lanes].astype(jnp.float32)
            ext[pl.ds(EDGE + frames, EDGE), :] = halo[1, u, :, lanes].astype(jnp.float32) * keep_right
            for start in range(0, frames, chunk):
                span = pl.ds(start, chunk)
                valid = valid_ref[u, span, :]
                linear = hidden_ref[u, span, lanes].astype(jnp.float32)
                gate = sigmoid(hidden_ref[u, span, gate_lanes].astype(jnp.float32))
                glu = (linear * gate * valid).astype(jnp.bfloat16).astype(jnp.float32)
                gated[...] = gate
                total = jnp.zeros((chunk, LANES), jnp.float32)
                for tap in range(taps):
                    moved = ext[pl.ds(start + EDGE + half - tap, chunk), :]
                    total = total + moved * taps_ref[pl.ds(tap, 1), lanes]
                    product = glu * moved
                    terms[tap] += sum(product[i : i + 8] for i in range(0, chunk, 8))
                gate = gated[...]
                opened = total * valid * gate
                linear = hidden_ref[u, span, lanes].astype(jnp.float32)
                hidden_grad_ref[u, span, lanes] = opened.astype(jnp.bfloat16)
                hidden_grad_ref[u, span, gate_lanes] = (
                    opened * linear * (1.0 - gate)
                ).astype(jnp.bfloat16)
            return 0

        lax.fori_loop(0, groups, utterance, 0)
        term_ref[:, lanes] = jnp.sum(terms[...], axis=1)
        return 0

    if not reduce:
        for copy in edges:
            copy.wait()
        lax.fori_loop(0, blocks, conv_block, 0)
        sum_ref[...] = jnp.zeros_like(sum_ref)
        return

    total, sending, landing, send_sem, recv_sem = scratch
    parts, count, depth, columns = total.shape
    orders = orders_of(dp, seq)
    offsets = [count - (count >> s) for s in range(steps)]
    bases = [0] * parts
    copies = [[None] * steps for _ in range(parts)]

    tile = LANES * depth // math.gcd(LANES, depth)
    for part in range(parts):
        for first in range(0, width, tile):
            product = lax.dot_general(
                swished_ref[:, pl.ds(first, tile)], out_ref[:, pl.ds(part * columns, columns)],
                (((0,), (0,)), ((), ())), preferred_element_type=jnp.float32)
            for i in range(tile // depth):
                place = place_of(first // depth + i, orders[part])
                total[part, place] = product[i * depth : (i + 1) * depth]

        launch(part, 0, steps, count, orders, bases, offsets, bit_of, partner_of, copies,
               total, sending, landing, send_sem, recv_sem)

    for copy in edges:
        copy.wait()
    share = [0] * (steps + 1)
    weights = [2, 4, 4, 2]
    done = 0
    for step in range(1, steps + 1):
        todo = min(blocks - done, weights[step - 1] * blocks // 12 if step < min(steps, 4) else blocks - done)
        if todo > 0:
            lax.fori_loop(done, done + todo, conv_block, 0)
            done += todo
        for part in range(parts):
            copies[part][step - 1].wait_recv()
            size = count >> step
            base, offset = bases[part], offsets[step - 1]
            if step < steps:
                def add(i, _, part=part, base=base, offset=offset):
                    total[part, base + i] += landing[part, offset + i].astype(jnp.float32)
                    return 0

                lax.fori_loop(0, size, add, 0)
                launch(part, step, steps, count, orders, bases, offsets, bit_of, partner_of, copies,
                       total, sending, landing, send_sem, recv_sem)
            else:
                sum_ref[:, pl.ds(part * columns, columns)] = factor * (
                    total[part, base] + landing[part, offset].astype(jnp.float32))
    for part in range(parts):
        for copy in copies[part]:
            copy.wait_send()


def launch(part, step, steps, count, orders, bases, offsets, bit_of, partner_of, copies,
           total, sending, landing, send_sem, recv_sem):
    bit = orders[part][step]
    size = count >> (step + 1)
    mine = bit_of(bit)
    away = bases[part] + (1 - mine) * size
    bases[part] = bases[part] + mine * size
    offset = offsets[step]

    def fill(i, _):
        sending[part, offset + i] = total[part, away + i].astype(jnp.bfloat16)
        return 0

    lax.fori_loop(0, size, fill, 0)
    copy = pltpu.make_async_remote_copy(
        sending.at[part, pl.ds(offset, size)], landing.at[part, pl.ds(offset, size)],
        send_sem.at[part, step], recv_sem.at[part, step],
        device_id=partner_of(bit), device_id_type=MESH)
    copy.start()
    copies[part][step] = copy


def backward(hidden, grad, swished, grad_out, valid, taps_rows, taps, dp, seq, reduce, factor):
    groups, frames, double = hidden.shape
    width = double // 2
    count = dp * seq
    depth = width // count
    parts = 3
    columns = width // parts
    steps = count.bit_length() - 1
    scratch = [
        pltpu.VMEM((frames + 2 * EDGE, LANES), jnp.float32),
        pltpu.VMEM((chunk_of(frames), LANES), jnp.float32),
        pltpu.VMEM((taps_rows.shape[0], 8, LANES), jnp.float32),
        pltpu.VMEM((2, groups, EDGE, width), jnp.bfloat16),
        pltpu.SemaphoreType.DMA((2, groups)),
        pltpu.SemaphoreType.DMA((2, groups)),
    ]
    if reduce:
        scratch += [
            pltpu.VMEM((parts, count, depth, columns), jnp.float32),
            pltpu.VMEM((parts, count, depth, columns), jnp.bfloat16),
            pltpu.VMEM((parts, count, depth, columns), jnp.bfloat16),
            pltpu.SemaphoreType.DMA((parts, steps)),
            pltpu.SemaphoreType.DMA((parts, steps)),
        ]
    vmem = pl.BlockSpec(memory_space=pltpu.VMEM)
    return pl.pallas_call(
        functools.partial(backward_kernel, taps, dp, seq, reduce, factor),
        in_specs=[vmem] * 6,
        out_specs=[vmem] * 3,
        out_shape=[
            jax.ShapeDtypeStruct(hidden.shape, jnp.bfloat16),
            jax.ShapeDtypeStruct((depth if reduce else 8, width), jnp.float32),
            jax.ShapeDtypeStruct((taps_rows.shape[0], width), jnp.float32),
        ],
        scratch_shapes=scratch,
        compiler_params=pltpu.CompilerParams(
            vmem_limit_bytes=VMEM_LIMIT, collective_id=0, has_side_effects=True),
    )(hidden, grad, swished, grad_out, valid, taps_rows)


def small_kernel(dp, seq, terms_ref, out_ref, landing, send_sem, recv_sem):
    count = dp * seq
    my_dp, my_seq = lax.axis_index("dp"), lax.axis_index("seq")
    me = my_dp * seq + my_seq

    def device(step):
        index = lax.rem(me + step, count)
        return index, (index // seq, lax.rem(index, seq))

    barrier = pltpu.get_barrier_semaphore()

    def greet(step, _):
        pl.semaphore_signal(barrier, inc=1, device_id=device(step)[1], device_id_type=MESH)
        return 0

    lax.fori_loop(1, count, greet, 0)
    pl.semaphore_wait(barrier, count - 1)

    def copy(step):
        index, target = device(step)
        return pltpu.make_async_remote_copy(
            terms_ref.at[index], landing.at[step], send_sem.at[step], recv_sem.at[step],
            device_id=target, device_id_type=MESH)

    def start(step, _):
        copy(step).start()
        return 0

    lax.fori_loop(1, count, start, 0)
    landing[0] = terms_ref[me]

    def finish(step, _):
        copy(step).wait()
        return 0

    lax.fori_loop(1, count, finish, 0)

    def add(step, total):
        return total + landing[step].astype(jnp.float32)

    out_ref[...] = lax.fori_loop(0, count, add, jnp.zeros(out_ref.shape, jnp.float32))


def small_sum(terms, dp, seq):
    count = dp * seq
    vmem = pl.BlockSpec(memory_space=pltpu.VMEM)
    return pl.pallas_call(
        functools.partial(small_kernel, dp, seq),
        in_specs=[vmem],
        out_specs=vmem,
        out_shape=jax.ShapeDtypeStruct(terms.shape[1:], jnp.float32),
        scratch_shapes=[
            pltpu.VMEM(terms.shape, jnp.bfloat16),
            pltpu.SemaphoreType.DMA((count,)),
            pltpu.SemaphoreType.DMA((count,)),
        ],
        compiler_params=pltpu.CompilerParams(collective_id=1, has_side_effects=True),
    )(terms)


def local(dp, seq, hidden, cotangent, lengths, kernel, conv_gain, w_out):
    groups, frames, double = hidden.shape
    width = double // 2
    taps = kernel.shape[1]
    rows = groups * frames
    count = dp * seq
    depth = width // count
    factor = 1.0 / math.sqrt(groups * dp * frames * seq)
    reduce = count & (count - 1) == 0 and depth % 16 == 0 and seq > 1 and dp > 1

    first = lax.axis_index("seq") * frames
    valid = (first + jnp.arange(frames, dtype=jnp.int32))[None, :] < lengths[:, None]
    valid_lanes = jnp.broadcast_to(valid.astype(jnp.float32)[:, :, None], (groups, frames, LANES))
    pad = -taps % 8
    taps_rows = jnp.pad(kernel.T, ((0, pad), (0, 0)))

    def gated_edge(start):
        cells = hidden[:, start : start + EDGE].astype(jnp.float32)
        here = valid[:, start : start + EDGE, None].astype(jnp.float32)
        return (cells[..., :width] * sigmoid(cells[..., width:]) * here).astype(jnp.bfloat16)

    left = lax.ppermute(gated_edge(frames - EDGE), "seq", [(i, i + 1) for i in range(seq - 1)])
    right = lax.ppermute(gated_edge(0), "seq", [(i + 1, i) for i in range(seq - 1)])

    grad_out = (cotangent * valid.astype(jnp.bfloat16)[:, :, None]).reshape(rows, width)
    upstream = lax.dot_general(
        grad_out, w_out, (((1,), (1,)), ((), ())), preferred_element_type=jnp.float32)

    swished, grad_conv, term_conv = forward(
        hidden, left, right, valid_lanes, taps_rows, conv_gain.reshape(1, width), upstream, taps)
    grad_hidden, sum_out, term_kernel = backward(
        hidden, grad_conv.reshape(groups, frames, width), swished, grad_out, valid_lanes, taps_rows,
        taps, dp, seq, reduce, factor)

    small = jnp.concatenate([term_kernel[:taps], jnp.sum(term_conv, axis=0, keepdims=True)], axis=0).T
    each = depth * (taps + 1)
    if reduce and each % LANES == 0:
        cells = small.astype(jnp.bfloat16).reshape(count, each // LANES, LANES)
        cells = jnp.pad(cells, ((0, 0), (0, -(each // LANES) % 16), (0, 0)))
        small = small_sum(cells, dp, seq)[: each // LANES].reshape(depth, taps + 1)
    else:
        small = lax.psum_scatter(small, ("dp", "seq"), scatter_dimension=0, tiled=True)
    if not reduce:
        term_out = lax.dot_general(
            swished, grad_out, (((0,), (0,)), ((), ())), preferred_element_type=jnp.float32)
        sum_out = factor * lax.psum_scatter(term_out, ("dp", "seq"), scatter_dimension=0, tiled=True)
    small = small * factor
    return (grad_hidden, sum_out, small[:, :taps], small[:, taps])


def solution(mesh):
    in_specs = (P("dp", "seq", None), P("dp", "seq", None), P("dp"), P(), P(), P())
    out_specs = (
        P("dp", "seq", None),
        P(("dp", "seq"), None),
        P(("dp", "seq"), None),
        P(("dp", "seq")),
    )
    return jax.shard_map(
        functools.partial(local, mesh.shape["dp"], mesh.shape["seq"]),
        mesh=mesh, in_specs=in_specs, out_specs=out_specs, check_vma=False)
```

time: 303 us -> 102 us (0.34)
  waiting for transfers between devices: 171 us -> 0.01 us
  Pallas kernels: 0 us -> 77.9 us
  other arithmetic: 46.5 us -> 3.04 us
  blocking collectives: 41.3 us -> 0 us
  between operations: 14.6 us -> 0.79 us
  starting transfers between devices: 10.4 us -> 3.65 us
  matrix products: 11.5 us -> 6.21 us
    reduce_scatter x1 -> x0, waiting for transfers between devices: 139 us -> none  [local(): lax.psum_scatter(term_out, ('dp', 'seq'), scatter_dimension=0, tiled=True)]
    pallas_call x0 -> x3, Pallas kernels: none -> 77.9 us  [the longest x1 45.6 us: backward(): pl.pallas_call(functools.partial(backward_kernel, taps, dp, seq, reduce,...]
    unnamed x1 -> x0, blocking collectives: 41.3 us -> none
    unnamed x3 -> x0, waiting for transfers between devices: 29.6 us -> none
    reduce_sum x4 -> x1, other arithmetic: 23.1 us -> 0.03 us  [local(): jnp.sum(term_conv, axis=0, keepdims=True)]
    add x2 -> x1, other arithmetic: 9.02 us -> 0.01 us  [local(): first + jnp.arange(frames, dtype=jnp.int32)]
    ppermute x4 -> x2, starting transfers between devices: 10.1 us -> 3.65 us  [the longest x1 2.36 us: local(): lax.ppermute(gated_edge(frames - EDGE), 'seq', [(i, i + 1) for i in range...]
    mul x5 -> x2, other arithmetic: 6.2 us -> 0.85 us  [the longest x1 0.7 us: local(): small = small * factor]
  transfers between devices with their start and end apart: 6 -> 2, of which waited for: 3 -> 0; matrix products, arithmetic and copies ran while one was open for 8% -> 8% of each run, Pallas kernels for 0% -> 0%
where the time goes in v1:
time: 102 us; the launch traced here: 101 us
  Pallas kernels  77.9 us (76%)
  local copies, waits for them, and re-layouts  9.65 us (9%)
  matrix products  6.21 us (6%)
  starting transfers between devices  3.65 us (4%)
  other arithmetic  3.04 us (3%)
    pallas_call x1, Pallas kernels, backward(): pl.pallas_call(functools.partial(backward_kernel, taps, dp, seq, reduce,...  45.6 us
    pallas_call x1, Pallas kernels, forward(): pl.pallas_call(functools.partial(forward_kernel, taps), grid=(blocks,), i...  19.7 us
    pallas_call x1, Pallas kernels, small_sum(): pl.pallas_call(functools.partial(small_kernel, dp, seq), in_specs=[vmem],...  12.6 us
    dot_general x1, matrix products, local(): lax.dot_general(grad_out, w_out, (((1,), (1,)), ((), ())), preferred_elem...  6.21 us
    unnamed x19, local copies, waits for them, and re-layouts  4.7 us
    ppermute x1, starting transfers between devices, local(): lax.ppermute(gated_edge(frames - EDGE), 'seq', [(i, i + 1) for i in range...  2.36 us
  transfers between devices with their start and end apart: 2, of which 0 were waited for; matrix products, arithmetic and copies ran while one was open for 8% of the time, Pallas kernels for 0%

profile of v1, /device:TPU:0, one launch (start us, length us, event | category | flops | bytes accessed | tf_op | source)
XLA Modules:
  0.0 101.3 jit_solution(10409719025640752474)
XLA Ops:
  0.7 0.8 fusion.12
  1.5 0.1 slice_convert_fusion.3
  1.6 1.1 %slice_convert_fusion.1 = (f32[2,16,3072]{2,1,0:T(8,128)S(1)}, f32[2,16,3072]{2,1,0:T(8,128)S(1)}) fusion(bf16[2,192,3072]{2,1,0:T(8,128)(2,1)} %hidden_ref.1), kind=kLoop, calls=%fused_computation.14 | loop fusion | flops 196608 | bytes 1179648 | tf_op jit(solution)/shard_map/convert_element_type | solution.py:412
  2.6 0.1 fusion.10
  2.7 2.4 %collective-permute-start = (bf16[2,16,1536]{2,1,0:T(8,128)(2,1)S(1)}, bf16[2,16,1536]{2,1,0:T(8,128)(2,1)S(1)}, u32[]{:S(2)}, u32[]{:S(2)}) collective-permute-start(bf16[2,16,1536]{2,1,0:T(8,128)(2,1)S(1)} %fusion.10), channel_id=1, source_target_pairs={{0,1},{1,2},{2,3},{3,4},{4,5},{5,6},{6,7},{8,9},{9,10},{10,11},{11... | collective-permute-start | bytes 294920 | tf_op jit(solution)/shard_map/ppermute | solution.py:416
  5.1 0.1 fusion.11
  5.2 1.3 %collective-permute-start.1 = (bf16[2,16,1536]{2,1,0:T(8,128)(2,1)S(1)}, bf16[2,16,1536]{2,1,0:T(8,128)(2,1)S(1)}, u32[]{:S(2)}, u32[]{:S(2)}) collective-permute-start(bf16[2,16,1536]{2,1,0:T(8,128)(2,1)S(1)} %fusion.11), channel_id=1, source_target_pairs={{1,0},{2,1},{3,2},{4,3},{5,4},{6,5},{7,6},{9,8},{10,9},{11,10},{12... | collective-permute-start | bytes 294920 | tf_op jit(solution)/shard_map/ppermute | solution.py:417
  6.5 0.1 broadcast_multiply_fusion
  6.7 6.2 %fusion.13.up_ref = f32[384,1536]{1,0:T(8,128)} fusion(bf16[384,1536]{1,0:T(8,128)(2,1)S(1)} %bitcast.8, bf16[1536,1536]{1,0:T(8,128)(2,1)} %param.11), kind=kOutput, calls=%fused_computation.26 | convolution fusion | flops 1811939328 | bytes 8257536 | tf_op jit(solution)/shard_map/dot_general | solution.py:420
  12.9 0.6 reshape.85.gain_ref
  13.5 0.7 pad.8.taps_ref
  14.2 0.8 broadcast_in_dim.5.valid_ref
  15.0 19.7 %shard_map.93 = (bf16[384,1536]{1,0:T(8,128)(2,1)}, bf16[384,1536]{1,0:T(8,128)(2,1)}, f32[8,1536]{1,0:T(8,128)}) custom-call(bf16[2,192,3072]{2,1,0:T(8,128)(2,1)} %hidden_ref.1, bf16[2,192,3072]{2,1,0:T(8,128)(2,1)} %hidden_ref.1, bf16[2,16,1536]{2,1,0:T(8,128)(2,1)} %copy-done.4, bf16[2,16,1536]{2,1,0:T(8,128)(2,1)} %copy-done.5, ...), custom_call_target="tpu_custom_call" | custom-call | tf_op jit(solution)/shard_map/pallas_call | solution.py:96
  34.7 45.6 %shard_map.94 = (bf16[2,192,3072]{2,1,0:T(8,128)(2,1)}, f32[48,1536]{1,0:T(8,128)}, f32[32,1536]{1,0:T(8,128)}) custom-call(bf16[2,192,3072]{2,1,0:T(8,128)(2,1)} %hidden_ref.1, bf16[2,192,1536]{2,1,0:T(8,128)(2,1)} %bitcast.10, bf16[384,1536]{1,0:T(8,128)(2,1)} %get-tuple-element.11.swished_ref, bf16[384,1536]{1,0:T(8,128)(2,1)} %bitcast.9, ...), custom_call_target="tpu_custom_call" | custom-call | tf_op jit(solution)/shard_map/pallas_call | solution.py:320
  80.4 0.9 slice.97
  81.4 0.2 copy.15
  81.6 0.2 reshape.88
  81.9 0.7 pad.9.terms_ref
  82.5 12.6 %shard_map.95 = f32[16,128]{1,0:T(8,128)} custom-call(bf16[32,16,128]{2,1,0:T(8,128)(2,1)} %pad.9.terms_ref), custom_call_target="tpu_custom_call" | custom-call | tf_op jit(solution)/shard_map/pallas_call | solution.py:381
  95.1 0.7 slice_multiply_fusion
  95.9 0.7 slice_reduce_fusion
  96.6 0.7 copy.16
  97.3 3.3 %copy.19 = bf16[2,192,3072]{2,1,0:T(8,128)(2,1)} copy(bf16[2,192,3072]{2,1,0:T(8,128)(2,1)} %get-tuple-element.34) | data formatting | bytes 4718592
  100.6 0.7 copy.20
  (24 shorter events, 0.2 us)
Async XLA Ops:
  0.6 5.8 %copy-start.1 = (bf16[2,192,1536]{2,1,0:T(8,128)(2,1)S(1)}, bf16[2,192,1536]{2,1,0:T(8,128)(2,1)}, u32[]{:S(2)}) copy-start(bf16[2,192,1536]{2,1,0:T(8,128)(2,1)} %param.7) | copy-start | bytes 3538948
  2.7 11.5 %collective-permute-start = (bf16[2,16,1536]{2,1,0:T(8,128)(2,1)S(1)}, bf16[2,16,1536]{2,1,0:T(8,128)(2,1)S(1)}, u32[]{:S(2)}, u32[]{:S(2)}) collective-permute-start(bf16[2,16,1536]{2,1,0:T(8,128)(2,1)S(1)} %fusion.10), channel_id=1, source_target_pairs={{0,1},{1,2},{2,3},{3,4},{4,5},{5,6},{6,7},{8,9},{9,10},{10,11},{11... | collective-permute-start | bytes 294920 | tf_op jit(solution)/shard_map/ppermute | solution.py:416
  5.2 9.0 %collective-permute-start.1 = (bf16[2,16,1536]{2,1,0:T(8,128)(2,1)S(1)}, bf16[2,16,1536]{2,1,0:T(8,128)(2,1)S(1)}, u32[]{:S(2)}, u32[]{:S(2)}) collective-permute-start(bf16[2,16,1536]{2,1,0:T(8,128)(2,1)S(1)} %fusion.11), channel_id=1, source_target_pairs={{1,0},{2,1},{3,2},{4,3},{5,4},{6,5},{7,6},{9,8},{10,9},{11,10},{12... | collective-permute-start | bytes 294920 | tf_op jit(solution)/shard_map/ppermute | solution.py:417
  6.6 6.2 %copy-start = (bf16[2,192,1536]{2,1,0:T(8,128)(2,1)}, bf16[2,192,1536]{2,1,0:T(8,128)(2,1)S(1)}, u32[]{:S(2)}) copy-start(bf16[2,192,1536]{2,1,0:T(8,128)(2,1)S(1)} %broadcast_multiply_fusion) | copy-start | bytes 3538948
  6.6 6.2 %copy-start.7 = (f32[1536]{0:T(1024)S(1)}, f32[1536]{0:T(1024)}, u32[]{:S(2)}) copy-start(f32[1536]{0:T(1024)} %param.10) | copy-start | bytes 18436
  6.7 6.8 %copy-start.3 = (f32[1536,31]{0,1:T(8,128)S(1)}, f32[1536,31]{0,1:T(8,128)}, u32[]{:S(2)}) copy-start(f32[1536,31]{0,1:T(8,128)} %param.9) | copy-start | bytes 571396
  14.2 0.8 copy-start.4
  14.2 0.8 copy-start.5
  34.7 45.7 %copy-start.6 = (f32[8,1536]{1,0:T(8,128)S(1)}, f32[8,1536]{1,0:T(8,128)}, u32[]{:S(2)}) copy-start(f32[8,1536]{1,0:T(8,128)} %get-tuple-element.15) | copy-start | bytes 147460
  97.3 3.3 %copy-start.2 = (f32[48,1536]{1,0:T(8,128)S(1)}, f32[48,1536]{1,0:T(8,128)}, u32[]{:S(2)}) copy-start(f32[48,1536]{1,0:T(8,128)} %get-tuple-element.35) | copy-start | bytes 884740

commit v2 on v0

v2 whole, which is shorter than its diff:
```python
import functools
import math

import jax
import jax.numpy as jnp
from jax import lax
from jax.experimental import pallas as pl
from jax.experimental.pallas import tpu as pltpu
from jax.sharding import PartitionSpec as P

EPSILON = 1e-05
LANES = 128
EDGE = 16
MESH = pl.DeviceIdType.MESH
VMEM_LIMIT = 60 * 2**20


def sigmoid(x):
    return jax.nn.sigmoid(x)


def chunk_of(frames):
    return 64 if frames % 64 == 0 else 32 if frames % 32 == 0 else 16


def orders_of(dp, seq):
    seq_bits, dp_bits = seq.bit_length() - 1, dp.bit_length() - 1
    others = list(range(seq_bits, seq_bits + dp_bits)) + list(range(1, seq_bits))
    turns = (0, 1, dp_bits)
    return [[0] + others[t:] + others[:t] for t in turns]


def place_of(index, order):
    place = 0
    for bit in order:
        place = place * 2 + (index >> bit) % 2
    return place


def fused_kernel(taps, dp, seq, reduce, factor, plan, hidden_ref, cot_ref, w_ref, valid_ref, taps_ref, gain_ref,
                 hidden_grad_ref, sum_ref, small_ref, swished_ref, out_ref, w_here, upstream, conv, grad_ref,
                 term_conv, ext, gated, terms, rows_of_terms, edges, halo, w_sem, edge_send, edge_recv, *scratch):
    groups, frames, double = hidden_ref.shape
    width = double // 2
    blocks = width // LANES
    half = taps // 2
    chunk = chunk_of(frames)
    rows = groups * frames
    my_dp, my_seq = lax.axis_index("dp"), lax.axis_index("seq")
    right = (my_dp, lax.rem(my_seq + 1, seq))
    left = (my_dp, lax.rem(my_seq + seq - 1, seq))
    seq_bits, dp_bits = seq.bit_length() - 1, dp.bit_length() - 1
    steps = seq_bits + dp_bits if reduce else 0

    def bit_of(bit):
        if bit < seq_bits:
            return lax.rem(my_seq // (1 << bit), 2)
        return lax.rem(my_dp // (1 << (bit - seq_bits)), 2)

    def partner_of(bit):
        turn = 1 - 2 * bit_of(bit)
        if bit < seq_bits:
            return (my_dp, my_seq + (1 << bit) * turn)
        return (my_dp + (1 << (bit - seq_bits)) * turn, my_seq)

    def lanes_of(block, offset=0):
        return pl.ds(pl.multiple_of(block * LANES + offset, LANES), LANES)

    load_w = pltpu.make_async_copy(w_ref, w_here, w_sem)
    load_w.start()
    barrier = pltpu.get_barrier_semaphore()
    partners = [left, right] + [partner_of(b) for b in range(steps)]
    for device in partners:
        pl.semaphore_signal(barrier, inc=1, device_id=device, device_id_type=MESH)

    def gate_edges(block, _):
        lanes = lanes_of(block)
        for u in range(groups):
            for side, start in ((0, frames - EDGE), (1, 0)):
                span = pl.ds(start, EDGE)
                opened = sigmoid(hidden_ref[u, span, lanes_of(block, width)].astype(jnp.float32))
                cells = hidden_ref[u, span, lanes].astype(jnp.float32) * opened * valid_ref[u, span, :]
                edges[side, u, :, lanes] = cells.astype(jnp.bfloat16)
        return 0

    lax.fori_loop(0, blocks, gate_edges, 0)
    pl.semaphore_wait(barrier, len(partners))

    def exchange(turn, source):
        copies = []
        for side, device in ((0, right), (1, left)):
            for u in range(groups):
                copies.append(pltpu.make_async_remote_copy(
                    source(side, u), halo.at[turn, side, u], edge_send.at[turn, side, u],
                    edge_recv.at[turn, side, u], device_id=device, device_id_type=MESH))
        for copy in copies:
            copy.start()
        return copies

    first = exchange(0, lambda side, u: edges.at[side, u])
    keep_left = jnp.where(my_seq == 0, 0.0, 1.0).astype(jnp.float32)
    keep_right = jnp.where(my_seq == seq - 1, 0.0, 1.0).astype(jnp.float32)

    def mask(block, _):
        lanes = lanes_of(block)
        for u in range(groups):
            out_ref[pl.ds(u * frames, frames), lanes] = (
                cot_ref[u, :, lanes].astype(jnp.float32) * valid_ref[u]).astype(jnp.bfloat16)
        return 0

    lax.fori_loop(0, blocks, mask, 0)
    load_w.wait()
    wide = 2 * LANES if blocks % 2 == 0 else LANES

    def project(index, _):
        span = pl.ds(pl.multiple_of(index * wide, wide), wide)
        upstream[:, span] = lax.dot_general(
            out_ref[...], w_here[span, :], (((1,), (1,)), ((), ())), preferred_element_type=jnp.float32)
        return 0

    lax.fori_loop(0, width // wide, project, 0)
    for copy in first:
        copy.wait()

    def convolve(block, _):
        lanes = lanes_of(block)

        def utterance(u, _):
            opened = sigmoid(hidden_ref[u, :, lanes_of(block, width)].astype(jnp.float32))
            cells = hidden_ref[u, :, lanes].astype(jnp.float32) * opened * valid_ref[u]
            ext[pl.ds(0, EDGE), :] = halo[0, 0, u, :, lanes].astype(jnp.float32) * keep_left
            ext[pl.ds(EDGE, frames), :] = cells.astype(jnp.bfloat16).astype(jnp.float32)
            ext[pl.ds(EDGE + frames, EDGE), :] = halo[0, 1, u, :, lanes].astype(jnp.float32) * keep_right
            for start in range(0, frames, chunk):
                total = jnp.zeros((chunk, LANES), jnp.float32)
                for tap in range(taps):
                    total = total + ext[pl.ds(start + tap + EDGE - half, chunk), :] * taps_ref[
                        pl.ds(tap, 1), lanes]
                conv[block, u, pl.ds(start, chunk), :] = total
            return 0

        lax.fori_loop(0, groups, utterance, 0)
        return 0

    lax.fori_loop(0, blocks, convolve, 0)
    term_conv[...] = jnp.zeros_like(term_conv)
    inverse_width = 1.0 / width

    def normalise(index, _):
        u = index // (frames // EDGE)
        inner = pl.ds(pl.multiple_of(lax.rem(index, frames // EDGE) * EDGE, EDGE), EDGE)
        span = pl.ds(pl.multiple_of(index * EDGE, EDGE), EDGE)
        values = [conv[b, u, inner, :] for b in range(blocks)]
        mean = jnp.sum(sum(values), axis=-1, keepdims=True) * inverse_width
        values = [v - mean for v in values]
        square = jnp.sum(sum(v * v for v in values), axis=-1, keepdims=True) * inverse_width
        inverse = lax.rsqrt(square + EPSILON)
        one = jnp.zeros((EDGE, LANES), jnp.float32)
        two = jnp.zeros((EDGE, LANES), jnp.float32)
        for b in range(blocks):
            lanes = pl.ds(b * LANES, LANES)
            gain = gain_ref[:, lanes]
            hat = values[b] * inverse
            pre = hat * gain
            gate = sigmoid(pre)
            swished_ref[span, lanes] = (pre * gate).astype(jnp.bfloat16)
            grad_pre = upstream[span, lanes] * gate * (1.0 + pre * (1.0 - gate))
            product = grad_pre * hat
            term_conv[:, lanes] += product[:8] + product[8:]
            grad = grad_pre * gain
            one = one + grad
            two = two + grad * hat
            conv[b, u, inner, :] = grad
            values[b] = hat
        mean_one = jnp.sum(one, axis=-1, keepdims=True) * inverse_width
        mean_two = jnp.sum(two, axis=-1, keepdims=True) * inverse_width
        for b in range(blocks):
            lanes = pl.ds(b * LANES, LANES)
            result = inverse * (conv[b, u, inner, :] - mean_one - values[b] * mean_two)
            grad_ref[u, inner, lanes] = result.astype(jnp.bfloat16)
        return 0

    lax.fori_loop(0, rows // EDGE, normalise, 0)
    second = exchange(
        1, lambda side, u: grad_ref.at[u, pl.ds(0 if side else frames - EDGE, EDGE)])
    rows_of_terms[...] = jnp.zeros_like(rows_of_terms)
    rows_of_terms[pl.ds(taps, 1), :] = jnp.sum(term_conv[...], axis=0, keepdims=True)

    def conv_block(block, _):
        lanes = lanes_of(block)
        gate_lanes = lanes_of(block, width)
        terms[...] = jnp.zeros_like(terms)

        def utterance(u, _):
            ext[pl.ds(0, EDGE), :] = halo[1, 0, u, :, lanes].astype(jnp.float32) * keep_left
            ext[pl.ds(EDGE, frames), :] = grad_ref[u, :, lanes].astype(jnp.float32)
            ext[pl.ds(EDGE + frames, EDGE), :] = halo[1, 1, u, :, lanes].astype(jnp.float32) * keep_right
            for start in range(0, frames, chunk):
                span = pl.ds(start, chunk)
                valid = valid_ref[u, span, :]
                linear = hidden_ref[u, span, lanes].astype(jnp.float32)
                gate = sigmoid(hidden_ref[u, span, gate_lanes].astype(jnp.float32))
                glu = (linear * gate * valid).astype(jnp.bfloat16).astype(jnp.float32)
                gated[...] = gate
                total = jnp.zeros((chunk, LANES), jnp.float32)
                for tap in range(taps):
                    moved = ext[pl.ds(start + EDGE + half - tap, chunk), :]
                    total = total + moved * taps_ref[pl.ds(tap, 1), lanes]
                    product = glu * moved
                    terms[tap] += sum(product[i : i + 8] for i in range(0, chunk, 8))
                gate = gated[...]
                opened = total * valid_ref[u, span, :] * gate
                linear = hidden_ref[u, span, lanes].astype(jnp.float32)
                hidden_grad_ref[u, span, lanes] = opened.astype(jnp.bfloat16)
                hidden_grad_ref[u, span, gate_lanes] = (
                    opened * linear * (1.0 - gate)
                ).astype(jnp.bfloat16)
            return 0

        lax.fori_loop(0, groups, utterance, 0)
        rows_of_terms[pl.ds(0, taps), lanes] = jnp.sum(terms[...], axis=1)[:taps]
        return 0

    if not reduce:
        for copy in second:
            copy.wait()
        lax.fori_loop(0, blocks, conv_block, 0)
        sum_ref[...] = jnp.zeros_like(sum_ref)
        small_ref[...] = rows_of_terms[...]
        return

    total, sending, landing, tiny, tiny_sending, tiny_landing, send_sem, recv_sem = scratch
    parts, count, depth, columns = total.shape
    totals = [total.at[p] for p in range(parts)] + [tiny]
    sends = [sending.at[p] for p in range(parts)] + [tiny_sending]
    lands = [landing.at[p] for p in range(parts)] + [tiny_landing]
    orders = orders_of(dp, seq)
    orders.append(orders[0])
    bases = [0] * (parts + 1)
    copies = [[] for _ in range(parts + 1)]
    tile = LANES * depth // math.gcd(LANES, depth)

    def launch(part):
        step = len(copies[part])
        bit = orders[part][step]
        size = count >> (step + 1)
        mine = bit_of(bit)
        away = bases[part] + (1 - mine) * size
        bases[part] = bases[part] + mine * size
        offset = count - (count >> step)

        def fill(i, _):
            sends[part][offset + i] = totals[part][away + i].astype(jnp.bfloat16)
            return 0

        lax.fori_loop(0, size, fill, 0)
        copy = pltpu.make_async_remote_copy(
            sends[part].at[pl.ds(offset, size)], lands[part].at[pl.ds(offset, size)],
            send_sem.at[part, step], recv_sem.at[part, step],
            device_id=partner_of(bit), device_id_type=MESH)
        copy.start()
        copies[part].append(copy)

    def advance(part):
        step = len(copies[part])
        copies[part][step - 1].wait_recv()
        size = count >> step
        base, offset = bases[part], count - (count >> (step - 1))
        if step < steps:
            def add(i, _):
                totals[part][base + i] += lands[part][offset + i].astype(jnp.float32)
                return 0

            lax.fori_loop(0, size, add, 0)
            launch(part)
        else:
            value = factor * (totals[part][base] + lands[part][offset].astype(jnp.float32))
            if part < parts:
                sum_ref[:, pl.ds(part * columns, columns)] = value
            else:
                small_ref[...] = value

    for part in range(parts):
        for start in range(0, width, tile):
            product = lax.dot_general(
                swished_ref[:, pl.ds(start, tile)], out_ref[:, pl.ds(part * columns, columns)],
                (((0,), (0,)), ((), ())), preferred_element_type=jnp.float32)
            for i in range(tile // depth):
                total[part, place_of(start // depth + i, orders[part])] = product[
                    i * depth : (i + 1) * depth]
        launch(part)
    for copy in second:
        copy.wait()

    done = 0
    for number in range(len(plan)):
        upto = blocks if number == len(plan) - 1 else min(blocks, done + blocks * plan[number] // sum(plan))
        if upto > done:
            lax.fori_loop(done, upto, conv_block, 0)
            done = upto
        if number < len(plan) - 1:
            for part in range(parts):
                advance(part)
    for start in range(0, width, tile):
        turned = rows_of_terms[:, pl.ds(start, tile)].T
        for i in range(tile // depth):
            tiny[place_of(start // depth + i, orders[parts])] = turned[i * depth : (i + 1) * depth]
    launch(parts)
    left_over = [steps - len(copies[p]) + 1 for p in range(parts + 1)]
    while any(left_over):
        for part in [parts] + list(range(parts)):
            if left_over[part]:
                advance(part)
                left_over[part] -= 1
    for part in range(parts + 1):
        for copy in copies[part]:
            copy.wait_send()


def fused(hidden, cotangent, w_out, valid, taps_rows, gain, taps, dp, seq, reduce, factor):
    groups, frames, double = hidden.shape
    width = double // 2
    blocks = width // LANES
    rows = groups * frames
    count = dp * seq
    depth = width // count
    parts = 3
    columns = width // parts
    steps = count.bit_length() - 1
    small = -(-(taps + 1) // LANES) * LANES
    shared = [((rows, width), jnp.bfloat16)] * 2
    out_shape = [
        jax.ShapeDtypeStruct(hidden.shape, jnp.bfloat16),
        jax.ShapeDtypeStruct((depth if reduce else 8, width), jnp.float32),
        jax.ShapeDtypeStruct((depth, small) if reduce else (small, width), jnp.float32),
    ]
    scratch = [
        pltpu.VMEM((width, width), jnp.bfloat16),
        pltpu.VMEM((rows, width), jnp.float32),
        pltpu.VMEM((blocks, groups, frames, LANES), jnp.float32),
        pltpu.VMEM((groups, frames, width), jnp.bfloat16),
        pltpu.VMEM((8, width), jnp.float32),
        pltpu.VMEM((frames + 2 * EDGE, LANES), jnp.float32),
        pltpu.VMEM((chunk_of(frames), LANES), jnp.float32),
        pltpu.VMEM((taps_rows.shape[0], 8, LANES), jnp.float32),
        pltpu.VMEM((small, width), jnp.float32),
        pltpu.VMEM((2, groups, EDGE, width), jnp.bfloat16),
        pltpu.VMEM((2, 2, groups, EDGE, width), jnp.bfloat16),
        pltpu.SemaphoreType.DMA,
        pltpu.SemaphoreType.DMA((2, 2, groups)),
        pltpu.SemaphoreType.DMA((2, 2, groups)),
    ]
    if reduce:
        scratch = [pltpu.VMEM(*s) for s in shared] + scratch + [
            pltpu.VMEM((parts, count, depth, columns), jnp.float32),
            pltpu.VMEM((parts, count, depth, columns), jnp.bfloat16),
            pltpu.VMEM((parts, count, depth, columns), jnp.bfloat16),
            pltpu.VMEM((count, depth, small), jnp.float32),
            pltpu.VMEM((count, depth, small), jnp.bfloat16),
            pltpu.VMEM((count, depth, small), jnp.bfloat16),
            pltpu.SemaphoreType.DMA((parts + 1, steps)),
            pltpu.SemaphoreType.DMA((parts + 1, steps)),
        ]
    else:
        out_shape += [jax.ShapeDtypeStruct(*s) for s in shared]
    vmem = pl.BlockSpec(memory_space=pltpu.VMEM)
    plan = (3, 6, 3)
    return pl.pallas_call(
        functools.partial(fused_kernel, taps, dp, seq, reduce, factor, plan),
        in_specs=[vmem, vmem, pl.BlockSpec(memory_space=pl.ANY)] + [vmem] * 3,
        out_specs=[vmem] * len(out_shape),
        out_shape=out_shape,
        scratch_shapes=scratch,
        compiler_params=pltpu.CompilerParams(
            vmem_limit_bytes=VMEM_LIMIT, collective_id=0, has_side_effects=True),
    )(hidden, cotangent, w_out, valid, taps_rows, gain)


def local(dp, seq, hidden, cotangent, lengths, kernel, conv_gain, w_out):
    groups, frames, double = hidden.shape
    width = double // 2
    taps = kernel.shape[1]
    count = dp * seq
    depth = width // count
    factor = 1.0 / math.sqrt(groups * dp * frames * seq)
    reduce = count & (count - 1) == 0 and depth % 16 == 0 and seq > 1 and dp > 1

    first = lax.axis_index("seq") * frames
    valid = (first + jnp.arange(frames, dtype=jnp.int32))[None, :] < lengths[:, None]
    valid_lanes = jnp.broadcast_to(valid.astype(jnp.float32)[:, :, None], (groups, frames, LANES))
    taps_rows = jnp.pad(kernel.T, ((0, -taps % 8), (0, 0)))
    grad_hidden, sum_out, small, *rest = fused(
        hidden, cotangent, w_out, valid_lanes, taps_rows, conv_gain.reshape(1, width),
        taps, dp, seq, reduce, factor)
    if not reduce:
        swished, grad_out = rest
        term_out = lax.dot_general(
            swished, grad_out, (((0,), (0,)), ((), ())), preferred_element_type=jnp.float32)
        sum_out = factor * lax.psum_scatter(term_out, ("dp", "seq"), scatter_dimension=0, tiled=True)
        small = factor * lax.psum_scatter(
            small[: taps + 1].T, ("dp", "seq"), scatter_dimension=0, tiled=True)
    return (grad_hidden, sum_out, small[:, :taps], small[:, taps])


def solution(mesh):
    in_specs = (P("dp", "seq", None), P("dp", "seq", None), P("dp"), P(), P(), P())
    out_specs = (
        P("dp", "seq", None),
        P(("dp", "seq"), None),
        P(("dp", "seq"), None),
        P(("dp", "seq")),
    )
    return jax.shard_map(
        functools.partial(local, mesh.shape["dp"], mesh.shape["seq"]),
        mesh=mesh, in_specs=in_specs, out_specs=out_specs, check_vma=False)
```

time: 303 us -> 79.3 us (0.26)
  waiting for transfers between devices: 171 us -> 0 us
  Pallas kernels: 0 us -> 67 us
  other arithmetic: 46.5 us -> 0.73 us
  blocking collectives: 41.3 us -> 0 us
  between operations: 14.6 us -> 0.65 us
  matrix products: 11.5 us -> 0 us
  starting transfers between devices: 10.4 us -> 0 us
  local copies, waits for them, and re-layouts: 6.78 us -> 10.5 us
    reduce_scatter x1 -> x0, waiting for transfers between devices: 139 us -> none  [local(): lax.psum_scatter(term_out, ('dp', 'seq'), scatter_dimension=0, tiled=True)]
    pallas_call x0 -> x1, Pallas kernels: none -> 67 us  [fused(): pl.pallas_call(functools.partial(fused_kernel, taps, dp, seq, reduce, fac...]
    unnamed x1 -> x0, blocking collectives: 41.3 us -> none
    unnamed x3 -> x0, waiting for transfers between devices: 29.6 us -> none
    reduce_sum x4 -> x0, other arithmetic: 23.1 us -> none  [the longest x1 11.5 us: normalize(): centered = values - jnp.mean(values, axis=-1, keepdims=True)]
    dot_general x2 -> x0, matrix products: 11.5 us -> none  [the longest x1 6.64 us: inner_rows(): lax.dot_general(left_side, right_side, (((0,), (0,)), ((), ())), preferre...]
    ppermute x4 -> x0, starting transfers between devices: 10.1 us -> none  [the longest x2 7.52 us: extended(): lax.ppermute(tail, axis, [(i, (i + 1) % count) for i in range(ends)])]
    add x2 -> x1, other arithmetic: 9.02 us -> 0.01 us  [local(): first + jnp.arange(frames, dtype=jnp.int32)]
  transfers between devices with their start and end apart: 6 -> 0, of which waited for: 3 -> 0; matrix products, arithmetic and copies ran while one was open for 8% -> 0% of each run, Pallas kernels for 0% -> 0%
where the time goes in v2:
time: 79.3 us; the launch traced here: 79 us
  Pallas kernels  67 us (84%)
  local copies, waits for them, and re-layouts  10.5 us (13%)
    pallas_call x1, Pallas kernels, fused(): pl.pallas_call(functools.partial(fused_kernel, taps, dp, seq, reduce, fac...  67 us
    unnamed x5, local copies, waits for them, and re-layouts  5.41 us
    pad x1, local copies, waits for them, and re-layouts, local(): taps_rows = jnp.pad(kernel.T, ((0, -taps % 8), (0, 0)))  1.62 us

profile of v2, /device:TPU:0, one launch (start us, length us, event | category | flops | bytes accessed | tf_op | source)
XLA Modules:
  0.0 79.0 jit_solution(5883048595214296306)
XLA Ops:
  0.6 0.7 compare_convert_fusion
  1.4 0.8 %broadcast_in_dim.2.valid_ref = f32[2,192,128]{2,1,0:T(8,128)} broadcast(f32[2,192]{1,0:T(2,128)S(1)} %compare_convert_fusion), dimensions={0,1} | broadcast | bytes 198144 | tf_op jit(solution)/shard_map/broadcast_in_dim | solution.py:390
  2.2 1.6 %pad.4.taps_ref = f32[32,1536]{1,0:T(8,128)} pad(f32[31,1536]{1,0:T(8,128)} %bitcast.2, f32[]{:T(128)} %constant.8.clone.1), padding=0_1x0_0 | pad | bytes 387076 | tf_op jit(solution)/shard_map/jit(_pad)/pad | solution.py:391
  3.8 1.3 %reshape.44.gain_ref = f32[1,1536]{1,0:T(1,128)} reshape(f32[1536]{0:T(1024)} %param.10) | data formatting | bytes 12288 | tf_op jit(solution)/shard_map/reshape | solution.py:393
  5.1 67.0 %shard_map.93 = (bf16[2,192,3072]{2,1,0:T(8,128)(2,1)}, f32[48,1536]{1,0:T(8,128)}, f32[48,128]{1,0:T(8,128)}) custom-call(bf16[2,192,3072]{2,1,0:T(8,128)(2,1)} %hidden_ref.1, bf16[2,192,1536]{2,1,0:T(8,128)(2,1)} %cot_ref.1, bf16[1536,1536]{1,0:T(8,128)(2,1)} %w_ref.1, f32[2,192,128]{2,1,0:T(8,128)} %broadcast_in_dim.2.valid_ref, f32[32,1536]{1,0:T(8,128)} %pad.4.taps_ref, ...), custom_call_target="tpu_custom_call" | custom-call | tf_op jit(solution)/shard_map/pallas_call | solution.py:368
  72.1 1.4 %copy.11 = f32[48,31]{0,1:T(8,128)} copy(f32[48,31]{1,0:T(8,128)} %bitcast.3) | data formatting | bytes 11904
  73.6 1.4 %slice_reduce_fusion = f32[48]{0:T(128)} fusion(f32[48,128]{1,0:T(8,128)} %get-tuple-element.9), kind=kLoop, calls=%fused_computation | loop fusion | bytes 384 | tf_op jit(solution)/shard_map/slice | solution.py:402
  75.0 0.0 copy-start
  75.0 3.3 %copy.14 = bf16[2,192,3072]{2,1,0:T(8,128)(2,1)} copy(bf16[2,192,3072]{2,1,0:T(8,128)(2,1)} %get-tuple-element.22) | data formatting | bytes 4718592
  78.3 0.0 copy-done
  78.3 0.7 copy.15
  (1 shorter events, 0.0 us)
Async XLA Ops:
  75.0 3.3 %copy-start = (f32[48,1536]{1,0:T(8,128)S(1)}, f32[48,1536]{1,0:T(8,128)}, u32[]{:S(2)}) copy-start(f32[48,1536]{1,0:T(8,128)} %get-tuple-element.23) | copy-start | bytes 884740
